TPU v7x, 512 devices: a whole 4x4x16 slice. The times are simulated.
512 devices in a mesh: grid: 64 (over y, z), freq: 8 (over x, core).
Axes of the slice: x: 4, y: 4, z: 16, core: 2. Of those that a mesh axis runs over, the one named last changes fastest.
Arguments:
- bin_index: int32 [16], P('freq'), may hold values from 64 to 511
- microphones: float32 [3, 128], replicated, may hold values from -0.5 to 0.5
- grid_points: float32 [3, 262144], P(None, 'grid'), may hold values from -1 to 1
- cross_spectra: float32 [16, 2, 128, 128], P('freq'), may hold values from -1 to 3, as said below
- initial_strengths: float32 [262144], P('grid'), may hold values from 0.05 to 2
Outputs:
- strengths: float32 [262144], P('grid')
Inputs may be any that keep to these rules, and one draw needn't show every extreme that they name: `cross_spectra`: for every bin the real part is symmetric and the imaginary part antisymmetric.
All inputs are finite; a program needn't handle non-finite values.
Results may differ from a plain program's by a relative error of at most 0.0045.
Values sent between devices are 32-bit elements; how exact they have to be, the bound alone decides.
A program may use at most 64 MiB of HBM per device.

v0:
```python
import math

import jax
import jax.numpy as jnp
from jax import lax
from jax.sharding import PartitionSpec as P

ITERS = 2


HEIGHT = 2.5
REFERENCE_RANGE = 2.5
WAVE_STEP = 2.0 * math.pi * 25.0 / 343.0


def steer_all(bin_index, microphones, grid_points):
    delta_x = grid_points[0][None, :] - microphones[0][:, None]
    delta_y = grid_points[1][None, :] - microphones[1][:, None]
    delta_z = grid_points[2][None, :] + HEIGHT - microphones[2][:, None]
    distance = jnp.sqrt(delta_x * delta_x + delta_y * delta_y + delta_z * delta_z)
    wavenumber = bin_index.astype(jnp.float32) * WAVE_STEP
    phase_angle = wavenumber[:, None, None] * distance[None]
    amplitude = REFERENCE_RANGE / distance
    return jnp.concatenate(
        [amplitude * jnp.cos(phase_angle), -amplitude * jnp.sin(phase_angle)], axis=1
    ).astype(jnp.bfloat16)


def outgoing(gram_rows, mic_count):
    real_part = gram_rows[:, :mic_count, :mic_count] + gram_rows[:, mic_count:, mic_count:]
    imag_part = gram_rows[:, mic_count:, :mic_count] - gram_rows[:, :mic_count, mic_count:]
    return jnp.stack([real_part, imag_part], axis=1)


def incoming(summed, inverse):
    real_part = summed[:, 0]
    imag_part = summed[:, 1]
    return (real_part * inverse, imag_part * inverse)


def local(bin_index, microphones, grid_points, cross_spectra, initial_strengths):
    mic_count = microphones.shape[1]
    inverse = 1.0 / (grid_points.shape[1] * lax.axis_size("grid"))
    strengths = initial_strengths
    for iteration in range(ITERS):
        steering = steer_all(bin_index, microphones, grid_points)
        weighted = (steering * strengths[None, None, :]).astype(jnp.bfloat16)
        gram_rows = jnp.einsum(
            "bmg,bng->bmn", weighted, steering, preferred_element_type=jnp.float32
        )
        summed = lax.psum(outgoing(gram_rows, mic_count), "grid")
        model_real, model_imag = incoming(summed, inverse)
        residual_real = (cross_spectra[:, 0] - model_real).astype(jnp.bfloat16)
        residual_imag = (cross_spectra[:, 1] - model_imag).astype(jnp.bfloat16)
        operator = jnp.concatenate(
            [
                jnp.concatenate([residual_real, -residual_imag], axis=2),
                jnp.concatenate([residual_imag, residual_real], axis=2),
            ],
            axis=1,
        )
        applied = jnp.einsum("bmn,bng->bmg", operator, steering, preferred_element_type=jnp.float32)
        grad_term = jnp.sum(steering * applied, axis=(0, 1))
        gradient = -2.0 * inverse * lax.psum(grad_term, "freq")
        local_norm = jnp.sum(gradient * gradient)
        weighted_grad = (steering * gradient[None, None, :]).astype(jnp.bfloat16)
        direction_rows = jnp.einsum(
            "bmg,bng->bmn", weighted_grad, steering, preferred_element_type=jnp.float32
        )
        outgoing_rows = outgoing(direction_rows, mic_count)
        grad_norm = lax.psum(local_norm, "grid")
        direction_summed = lax.psum(outgoing_rows, "grid")
        direction_real, direction_imag = incoming(direction_summed, inverse)
        local_curvature = jnp.sum(direction_real * direction_real + direction_imag * direction_imag)
        curvature = lax.psum(local_curvature, "freq")
        step_length = 0.5 * grad_norm / curvature
        strengths = jnp.maximum(strengths - step_length * gradient, 0.0)
    return strengths


def solution(mesh):
    placed = (P("freq"), P(), P(None, "grid"), P("freq", None, None, None), P("grid"))
    return jax.shard_map(local, mesh=mesh, in_specs=placed, out_specs=P("grid"), check_vma=False)
```

profile of v0, /device:TPU:1, one launch (start us, length us, event | category | flops | bytes accessed | tf_op | source)
XLA Modules:
  0.0 1171.5 jit_solution(6514725706348589083)
XLA Ops:
  6.5 0.0 all-reduce.5.cloned.1.call-start
  6.5 0.7 convert_multiply_fusion.6
  7.2 0.8 slice_bitcast_fusion.2
  8.0 1.0 fusion.72
  9.0 1.2 rsqrt_multiply_fusion
  10.3 0.0 copy-start.2
  10.3 15.5 %fusion.15 = (bf16[2,128,4096]{2,1,0:T(8,128)(2,1)S(1)}, bf16[2,128,4096]{2,1,0:T(8,128)(2,1)S(1)}) fusion(f32[128,4096]{1,0:T(8,128)S(1)} %get-tuple-element.24, f32[2]{0:T(128)S(1)} %convert_multiply_fusion.6, f32[128,4096]{1,0:T(8,128)S(1)} %get-tuple-element.22, f32[128,4096]{1,0:T(8,128)S(1)} %get-tuple-element.23), kind=kLoop, calls=%fused_computation.19 | loop fusion | flops 5242880 | bytes 10485768 | tf_op jit(solution)/shard_map/convert
  25.8 0.0 copy-start
  25.8 0.0 copy-done.2
  25.8 0.0 copy-start.1
  25.8 1.3 fusion.12
  27.1 0.0 copy-done
  27.2 0.7 pad_maximum_fusion.1
  27.9 0.0 all-reduce.5.cloned.1.call-update
  27.9 0.0 all-reduce.7.cloned.1.call-start
  28.0 257.5 %all-reduce.5.cloned.1.call-done = f32[2,2,128,128]{3,2,0,1:T(8,128)} async-done(((f32[2,2,128,128]{3,2,0,1:T(8,128)}), f32[2,2,128,128]{3,2,0,1:T(8,128)}) %all-reduce.5.cloned.1.call-update) | async-done | bytes 262160 | tf_op jit(solution)/shard_map/psum | solution.py:51
  285.5 0.0 copy-done.1
  285.5 0.9 fusion.62
  286.4 0.9 fusion.70
  287.3 3.6 fusion.1
  290.9 31.2 %psum.71 = f32[4096]{0:T(1024)S(1)} all-reduce(f32[4096]{0:T(1024)S(1)} %fusion.1), channel_id=1, replica_groups=mesh['grid'=64,'freq'=8] {'freq'}, use_global_device_ids=true, to_apply=%region_2.0 | all-reduce | flops 4096 | bytes 32768 | tf_op jit(solution)/shard_map/psum | solution.py:64
  322.1 0.6 broadcast_multiply_fusion.1
  322.7 3.5 fusion.10
  326.3 0.7 pad_maximum_fusion.2
  327.0 0.0 all-reduce.7.cloned.1.call-update
  327.0 0.0 all-reduce.9.cloned.1.call-start
  327.1 113.0 %psum.72 = f32[]{:T(128)} all-reduce(f32[]{:T(128)} %get-tuple-element.28), channel_id=1, replica_groups=mesh['grid'=64,'freq'=8] {'grid'}, use_global_device_ids=true, to_apply=%region_4.0 | all-reduce | flops 1 | bytes 8 | tf_op jit(solution)/shard_map/psum | solution.py:71
  440.0 134.1 %all-reduce.7.cloned.1.call-done = f32[2,2,128,128]{3,2,0,1:T(8,128)} async-done(((f32[2,2,128,128]{3,2,0,1:T(8,128)}), f32[2,2,128,128]{3,2,0,1:T(8,128)}) %all-reduce.7.cloned.1.call-update) | async-done | bytes 262160 | tf_op jit(solution)/shard_map/psum | solution.py:72
  574.2 1.6 fusion.52
  576.4 23.5 %psum.74 = f32[]{:T(128)} all-reduce(f32[]{:T(128)} %fusion.52), channel_id=1, replica_groups=mesh['grid'=64,'freq'=8] {'freq'}, use_global_device_ids=true, to_apply=%region_7.0 | all-reduce | flops 1 | bytes 8 | tf_op jit(solution)/shard_map/psum | solution.py:75
  600.6 3.5 fusion.8
  604.2 0.7 pad_maximum_fusion.3
  604.9 0.0 all-reduce.9.cloned.1.call-update
  604.9 0.0 all-reduce.11.cloned.1.call-start
  605.0 244.2 %all-reduce.9.cloned.1.call-done = f32[2,2,128,128]{3,2,0,1:T(8,128)} async-done(((f32[2,2,128,128]{3,2,0,1:T(8,128)}), f32[2,2,128,128]{3,2,0,1:T(8,128)}) %all-reduce.9.cloned.1.call-update) | async-done | bytes 262160 | tf_op jit(solution)/shard_map/psum | solution.py:51
  849.2 0.9 fusion.64
  850.1 0.9 fusion.68
  851.0 3.6 fusion.4
  854.6 31.3 %psum.76 = f32[4096]{0:T(1024)S(1)} all-reduce(f32[4096]{0:T(1024)S(1)} %fusion.4), channel_id=1, replica_groups=mesh['grid'=64,'freq'=8] {'freq'}, use_global_device_ids=true, to_apply=%region_10.0 | all-reduce | flops 4096 | bytes 32768 | tf_op jit(solution)/shard_map/psum | solution.py:64
  885.8 0.6 broadcast_multiply_fusion
  886.4 3.5 fusion.6
  890.0 0.7 pad_maximum_fusion.4
  890.7 0.0 all-reduce.11.cloned.1.call-update
  890.7 112.9 %psum.77 = f32[]{:T(128)} all-reduce(f32[]{:T(128)} %get-tuple-element.26), channel_id=1, replica_groups=mesh['grid'=64,'freq'=8] {'grid'}, use_global_device_ids=true, to_apply=%region_12.0 | all-reduce | flops 1 | bytes 8 | tf_op jit(solution)/shard_map/psum | solution.py:71
  1003.7 134.2 %all-reduce.11.cloned.1.call-done = f32[2,2,128,128]{3,2,0,1:T(8,128)} async-done(((f32[2,2,128,128]{3,2,0,1:T(8,128)}), f32[2,2,128,128]{3,2,0,1:T(8,128)}) %all-reduce.11.cloned.1.call-update) | async-done | bytes 262160 | tf_op jit(solution)/shard_map/psum | solution.py:72
  1137.8 1.7 fusion.40
  1140.1 23.5 %psum.79 = f32[]{:T(128)} all-reduce(f32[]{:T(128)} %fusion.40), channel_id=1, replica_groups=mesh['grid'=64,'freq'=8] {'freq'}, use_global_device_ids=true, to_apply=%region_15.0 | all-reduce | flops 1 | bytes 8 | tf_op jit(solution)/shard_map/psum | solution.py:75
  1164.3 0.6 subtract_maximum_fusion
  (5 shorter events, 0.1 us)
Async XLA Ops:
  6.5 278.9 %all-reduce.5.cloned.1.call-start = ((), (), s32[]{:S(2)}) async-start(), calls=%async_computation | async-start | bytes 524288 | tf_op jit(solution)/shard_map/psum | solution.py:51
  10.3 15.5 %copy-start.2 = (f32[4096]{0:T(1024)S(1)}, f32[4096]{0:T(1024)}, u32[]{:S(2)}) copy-start(f32[4096]{0:T(1024)} %param.9) | copy-start | bytes 49156
  25.8 1.4 copy-start
  25.8 259.7 %copy-start.1 = (f32[2,2,128,128]{3,2,1,0:T(8,128)S(1)}, f32[2,2,128,128]{3,2,1,0:T(8,128)}, u32[]{:S(2)}) copy-start(f32[2,2,128,128]{3,2,1,0:T(8,128)} %param.8) | copy-start | bytes 786436
  27.9 546.2 %all-reduce.7.cloned.1.call-start = ((), (), s32[]{:S(2)}) async-start(), calls=%async_computation.1 | async-start | bytes 524288 | tf_op jit(solution)/shard_map/psum | solution.py:72
  327.0 522.1 %all-reduce.9.cloned.1.call-start = ((), (), s32[]{:S(2)}) async-start(), calls=%async_computation.2 | async-start | bytes 524288 | tf_op jit(solution)/shard_map/psum | solution.py:51
  604.9 532.9 %all-reduce.11.cloned.1.call-start = ((), (), s32[]{:S(2)}) async-start(), calls=%async_computation.3 | async-start | bytes 524288 | tf_op jit(solution)/shard_map/psum | solution.py:72
Sparse Core Ops, SparseCore 0:
  28.0 257.3 all-reduce.4
  327.2 246.9 all-reduce.6
  605.0 244.0 all-reduce.8
  890.9 246.9 all-reduce.10
where the time goes:
time: 1170 us
  waiting for transfers between devices  770 us (66%)
  blocking collectives  335 us (29%)
  other arithmetic  30.2 us (3%)
  matrix products  18.9 us (2%)
  between operations  16 us (1%)
    psum x2, waiting for transfers between devices, local(): summed = lax.psum(outgoing(gram_rows, mic_count), 'grid')  502 us
    psum x2, waiting for transfers between devices, local(): direction_summed = lax.psum(outgoing_rows, 'grid')  268 us
    psum x2, blocking collectives, local(): grad_norm = lax.psum(local_norm, 'grid')  226 us
    psum x2, blocking collectives, local(): gradient = -2.0 * inverse * lax.psum(grad_term, 'freq')  62.5 us
    psum x2, blocking collectives, local(): curvature = lax.psum(local_curvature, 'freq')  47 us
  transfers between devices with their start and end apart: 4, of which 4 were waited for; matrix products, arithmetic and copies ran while one was open for 0% of the time, Pallas kernels for 0%

commit v1 on v0

v1 whole, which is shorter than its diff:
```python
import functools
import math

import jax
import jax.numpy as jnp
from jax import lax
from jax.experimental import pallas as pl
from jax.experimental.pallas import tpu as pltpu
from jax.sharding import PartitionSpec as P

ITERS = 2
GRID_Y = 4

HEIGHT = 2.5
REFERENCE_RANGE = 2.5
TURN_STEP = 25.0 / 343.0
HALF_PI = math.pi / 2.0

MESH = pl.DeviceIdType.MESH
F32 = jnp.float32
BF16 = jnp.bfloat16

SIN_COEFFS = (3.141590270, -5.167406733, 2.544010518, -0.559462455)
COS_COEFFS = (0.999993249, -4.933934668, 4.041248102, -1.222031763)


def horner(coeffs, u):
    value = coeffs[-1]
    for c in coeffs[-2::-1]:
        value = value * u + c
    return value


def kernel(
    grid_size,
    freq_size,
    bins_ref,
    mics_ref,
    points_ref,
    cross_ref,
    start_ref,
    out_ref,
    mic_cols,
    steer,
    gram,
    strength,
    ysend,
    yrecv,
    zsend,
    zrecv,
    gather,
    grads,
    parts_a,
    parts_b,
    send_sem,
    recv_sem,
):
    nb = bins_ref.shape[0]
    mics = mics_ref.shape[1]
    points = points_ref.shape[1]
    ny = GRID_Y
    nz = grid_size // ny
    rows_y = mics // ny
    rows_z = nb * rows_y // nz
    total = points * grid_size
    inverse = 1.0 / total

    g = lax.axis_index("grid")
    f = lax.axis_index("freq")
    y, z = lax.div(g, nz), lax.rem(g, nz)

    def at(y_id, z_id, f_id):
        return {"grid": y_id * nz + z_id, "freq": f_id}

    z_ids = [lax.rem(z + d, nz) for d in range(1, nz)]
    y_ids = [lax.rem(y + d, ny) for d in range(1, ny)]
    f_ids = [lax.rem(f + d, freq_size) for d in range(1, freq_size)]
    z_peers = [at(y, i, f) for i in z_ids]
    y_peers = [at(i, z, f) for i in y_ids]
    f_peers = [at(y, z, i) for i in f_ids]
    fy_peers = y_peers + f_peers + [at(i, z, j) for i in y_ids for j in f_ids]

    barrier = pltpu.get_barrier_semaphore()
    for peer in z_peers + fy_peers:
        pl.semaphore_signal(barrier, inc=1, device_id=peer, device_id_type=MESH)

    def send(phase, src, dst, peer):
        pltpu.make_async_remote_copy(
            src_ref=src,
            dst_ref=dst,
            send_sem=send_sem.at[phase],
            recv_sem=recv_sem.at[phase],
            device_id=peer,
            device_id_type=MESH,
        ).start()

    def arrive(phase, like):
        pltpu.make_async_copy(like, like, recv_sem.at[phase]).wait()

    def sent(phase, like):
        pltpu.make_async_copy(like, like, send_sem.at[phase]).wait()

    for axis in range(3):
        mic_cols[axis] = jnp.transpose(jnp.broadcast_to(mics_ref[axis : axis + 1, :], (mics, mics)))
    scale = [bins_ref[b].astype(F32) * TURN_STEP for b in range(nb)]
    sub, lanes = 16, 256
    blocks_m = mics // sub

    def steer_block(i, carry):
        m0 = pl.multiple_of(lax.rem(i, blocks_m) * sub, sub)
        c0 = pl.multiple_of(lax.div(i, blocks_m) * lanes, lanes)
        cols = pl.ds(c0, lanes)

        def mic(axis):
            tile = mic_cols[axis, pl.ds(m0, sub), :]
            return jnp.concatenate([tile] * (lanes // mics), axis=1)

        dx = points_ref[0:1, cols] - mic(0)
        dy = points_ref[1:2, cols] - mic(1)
        dz = (points_ref[2:3, cols] + HEIGHT) - mic(2)
        square = dx * dx + dy * dy + dz * dz
        inv = lax.rsqrt(square)
        inv = inv * (1.5 - 0.5 * square * inv * inv)
        distance = square * inv
        amplitude = REFERENCE_RANGE * inv
        for b in range(nb):
            turns = distance * scale[b]
            frac = turns - jnp.round(turns)
            u = frac * frac
            half_sin = frac * horner(SIN_COEFFS, u)
            half_cos = horner(COS_COEFFS, u)
            twice = (2.0 * amplitude) * half_sin
            real = amplitude - twice * half_sin
            imag = -(twice * half_cos)
            steer[b, pl.ds(m0, sub), cols] = real.astype(BF16)
            steer[b, pl.ds(m0 + mics, sub), cols] = imag.astype(BF16)
        return carry

    lax.fori_loop(0, blocks_m * (points // lanes), steer_block, 0)

    strength[...] = start_ref[...]

    row = lax.broadcasted_iota(jnp.int32, (mics, mics), 0)
    col = lax.broadcasted_iota(jnp.int32, (mics, mics), 1)
    upper = row <= col
    diagonal = row == col

    chunk = 1024

    def gram_into(weights_of):
        gram[...] = jnp.zeros_like(gram)

        def step(k, carry):
            cols = pl.ds(pl.multiple_of(k * chunk, chunk), chunk)
            w = weights_of(cols)
            for b in range(nb):
                s = steer[b, :, cols]
                weighted = (s.astype(F32) * w).astype(BF16)
                gram[b] += lax.dot_general(
                    weighted, s, (((1,), (1,)), ((), ())), preferred_element_type=F32
                )
            return carry

        lax.fori_loop(0, points // chunk, step, 0)

    def packed(b):
        real = gram[b, :mics, :mics] + gram[b, mics:, mics:]
        imag = gram[b, mics:, :mics] - gram[b, :mics, mics:]
        return jnp.where(upper, real, imag)

    def reduce_scatter(it, which):
        slot = 2 * it + which
        phase = 8 * it + 4 * which
        for b in range(nb):
            full = packed(b)
            for j in range(ny):
                ysend[slot, j, b] = full[j * rows_y : (j + 1) * rows_y, :]
        for d, peer in enumerate(y_peers):
            send(phase, ysend.at[slot, y_ids[d]], yrecv.at[slot, d], peer)
        arrive(phase, yrecv.at[slot])
        part = ysend[slot, y]
        for d in range(ny - 1):
            part = part + yrecv[slot, d]
        zsend[slot] = part.reshape(nz, rows_z, mics)
        for d, peer in enumerate(z_peers):
            send(phase + 1, zsend.at[slot, z_ids[d]], zrecv.at[slot, d], peer)
        arrive(phase + 1, zrecv.at[slot])
        mine = zsend[slot, z]
        for d in range(nz - 1):
            mine = mine + zrecv[slot, d]
        return mine

    for it in range(ITERS):
        gram_into(lambda cols: strength[:, cols])
        if it == 0:
            pl.semaphore_wait(barrier, len(z_peers) + len(fy_peers))
        mine = reduce_scatter(it, 0)
        gather[it, y, z] = mine
        for peer in z_peers:
            send(8 * it + 2, gather.at[it, y, z], gather.at[it, y, z], peer)
        arrive(8 * it + 2, gather.at[it, 0, pl.ds(0, nz - 1)])
        for peer in y_peers:
            send(8 * it + 3, gather.at[it, y], gather.at[it, y], peer)
        arrive(8 * it + 3, gather.at[it, pl.ds(0, ny - 1)])
        operators = []
        for b in range(nb):
            model = jnp.concatenate(
                [gather[it, j].reshape(nb, rows_y, mics)[b] for j in range(ny)], axis=0
            )
            flipped = jnp.transpose(model)
            model_real = jnp.where(upper, model, flipped)
            model_imag = jnp.where(diagonal, 0.0, jnp.where(upper, -flipped, model))
            res_real = cross_ref[b, 0] - model_real * inverse
            res_imag = cross_ref[b, 1] - model_imag * inverse
            operators.append(
                jnp.concatenate(
                    [
                        jnp.concatenate([res_real, -res_imag], axis=1),
                        jnp.concatenate([res_imag, res_real], axis=1),
                    ],
                    axis=0,
                ).astype(BF16)
            )

        width = 512
        for k in range(points // width):
            cols = pl.ds(k * width, width)
            term = None
            for b in range(nb):
                s = steer[b, :, cols]
                applied = jnp.dot(operators[b], s, preferred_element_type=F32)
                product = (s.astype(F32) * applied).reshape(2 * mics // 8, 8, width)
                product = jnp.sum(product, axis=0)
                term = product if term is None else term + product
            grads[it, f, :, cols] = jnp.sum(term, axis=0, keepdims=True)
        for peer in f_peers:
            send(16 + it, grads.at[it, f], grads.at[it, f], peer)
        arrive(16 + it, grads.at[it, pl.ds(0, freq_size - 1)])
        gradient = grads[it, 0]
        for j in range(1, freq_size):
            gradient = gradient + grads[it, j]
        gradient = (-2.0 * inverse) * gradient
        grads[it, freq_size] = gradient

        gram_into(lambda cols: grads[it, freq_size, :, cols])
        mine = reduce_scatter(it, 1) * inverse
        index = lax.broadcasted_iota(jnp.int32, (rows_z, mics), 0) + z * rows_z
        index = lax.rem(index, rows_y) + y * rows_y
        column = lax.broadcasted_iota(jnp.int32, (rows_z, mics), 1)
        curved = jnp.sum(mine * mine * jnp.where(index == column, 1.0, 2.0), axis=0, keepdims=True)
        squares = gradient * gradient
        normed = squares[:, :mics]
        for k in range(1, points // mics):
            normed = normed + squares[:, k * mics : (k + 1) * mics]
        own = y * freq_size + f
        parts_a[it, own] = jnp.concatenate([normed * (1.0 / freq_size), curved], axis=0)
        for peer in fy_peers:
            send(18 + 2 * it, parts_a.at[it, own], parts_a.at[it, own], peer)
        arrive(18 + 2 * it, parts_a.at[it, pl.ds(0, ny * freq_size - 1)])
        parts_b[it, z] = jnp.sum(parts_a[it], axis=0)
        for peer in z_peers:
            send(19 + 2 * it, parts_b.at[it, z], parts_b.at[it, z], peer)
        arrive(19 + 2 * it, parts_b.at[it, pl.ds(0, nz - 1)])
        sums = jnp.sum(jnp.sum(parts_b[it], axis=0), axis=1, keepdims=True)
        step_length = 0.5 * sums[0:1] / sums[1:2]
        updated = jnp.maximum(strength[...] - step_length * gradient, 0.0)
        if it < ITERS - 1:
            strength[...] = updated
        else:
            out_ref[...] = updated

    for it in range(ITERS):
        for which in range(2):
            slot, phase = 2 * it + which, 8 * it + 4 * which
            sent(phase, yrecv.at[slot])
            sent(phase + 1, zrecv.at[slot])
        sent(8 * it + 2, gather.at[it, 0, pl.ds(0, nz - 1)])
        sent(8 * it + 3, gather.at[it, pl.ds(0, ny - 1)])
        sent(16 + it, grads.at[it, pl.ds(0, freq_size - 1)])
        sent(18 + 2 * it, parts_a.at[it, pl.ds(0, ny * freq_size - 1)])
        sent(19 + 2 * it, parts_b.at[it, pl.ds(0, nz - 1)])


def local(grid_size, freq_size, bin_index, microphones, grid_points, cross_spectra, initial_strengths):
    nb = bin_index.shape[0]
    mics = microphones.shape[1]
    points = grid_points.shape[1]
    ny = GRID_Y
    nz = grid_size // ny
    rows_y = mics // ny
    rows_z = nb * rows_y // nz
    vmem = pl.BlockSpec(memory_space=pltpu.VMEM)
    out = pl.pallas_call(
        functools.partial(kernel, grid_size, freq_size),
        out_shape=jax.ShapeDtypeStruct((1, points), F32),
        in_specs=[pl.BlockSpec(memory_space=pltpu.SMEM), vmem, vmem, vmem, vmem],
        out_specs=vmem,
        scratch_shapes=[
            pltpu.VMEM((3, mics, mics), F32),
            pltpu.VMEM((nb, 2 * mics, points), BF16),
            pltpu.VMEM((nb, 2 * mics, 2 * mics), F32),
            pltpu.VMEM((1, points), F32),
            pltpu.VMEM((2 * ITERS, ny, nb, rows_y, mics), F32),
            pltpu.VMEM((2 * ITERS, ny - 1, nb, rows_y, mics), F32),
            pltpu.VMEM((2 * ITERS, nz, rows_z, mics), F32),
            pltpu.VMEM((2 * ITERS, nz - 1, rows_z, mics), F32),
            pltpu.VMEM((ITERS, ny, nz, rows_z, mics), F32),
            pltpu.VMEM((ITERS, freq_size + 1, 1, points), F32),
            pltpu.VMEM((ITERS, ny * freq_size, 2, mics), F32),
            pltpu.VMEM((ITERS, nz, 2, mics), F32),
            pltpu.SemaphoreType.DMA((22,)),
            pltpu.SemaphoreType.DMA((22,)),
        ],
        compiler_params=pltpu.CompilerParams(
            collective_id=0, has_side_effects=True, vmem_limit_bytes=40 * 1024 * 1024
        ),
        name="map_fit",
    )(bin_index, microphones, grid_points, cross_spectra, initial_strengths.reshape(1, points))
    return out.reshape(points)


def solution(mesh):
    placed = (P("freq"), P(), P(None, "grid"), P("freq", None, None, None), P("grid"))
    body = functools.partial(local, mesh.shape["grid"], mesh.shape["freq"])
    return jax.shard_map(body, mesh=mesh, in_specs=placed, out_specs=P("grid"), check_vma=False)
```

time: 1170 us -> 131 us (0.11)
  waiting for transfers between devices: 770 us -> 0 us
  blocking collectives: 335 us -> 0 us
  Pallas kernels: 0 us -> 126 us
  other arithmetic: 30.2 us -> 0 us
  matrix products: 18.9 us -> 0 us
  between operations: 16 us -> 0.01 us
    psum x4 -> x0, waiting for transfers between devices: 770 us -> none  [the longest x2 502 us: local(): summed = lax.psum(outgoing(gram_rows, mic_count), 'grid')]
    psum x6 -> x0, blocking collectives: 335 us -> none  [the longest x2 226 us: local(): grad_norm = lax.psum(local_norm, 'grid')]
    pallas_call x0 -> x1, Pallas kernels: none -> 126 us  [local(): pl.pallas_call(functools.partial(kernel, grid_size, freq_size), out_shape...]
    dot_general x6 -> x0, matrix products: 18.9 us -> none  [the longest x2 7.12 us: local(): jnp.einsum('bmn,bng->bmg', operator, steering, preferred_element_type=jnp...]
    another operation x9 -> x0, other arithmetic: 18.5 us -> none
  transfers between devices with their start and end apart: 4 -> 0, of which waited for: 4 -> 0; matrix products, arithmetic and copies ran while one was open for 0% -> 0% of each run, Pallas kernels for 0% -> 0%
where the time goes in v1:
time: 131 us
  Pallas kernels  126 us (96%)
  local copies, waits for them, and re-layouts  4.45 us (3%)
    pallas_call x1, Pallas kernels, local(): pl.pallas_call(functools.partial(kernel, grid_size, freq_size), out_shape...  126 us
    unnamed x11, local copies, waits for them, and re-layouts  4.45 us

profile of v1, /device:TPU:1, one launch (start us, length us, event | category | flops | bytes accessed | tf_op | source)
XLA Modules:
  0.0 130.8 jit_solution(12373959436109202856)
XLA Ops:
  0.0 0.0 copy-start.4
  0.0 0.7 copy-done.4
  0.7 0.0 copy-start
  0.7 0.9 copy-done
  1.6 0.0 copy-start.1
  1.6 0.8 copy-done.1
  2.4 0.0 copy-start.2
  2.4 0.7 copy-done.2
  3.2 0.0 copy-start.3
  3.2 0.7 copy-done.3
  3.8 126.3 %map_fit.1 = f32[1,4096]{1,0:T(1,128)S(1)} custom-call(s32[2]{0:T(128)S(1)} %copy-done.4, f32[3,128]{1,0:T(4,128)S(1)} %copy-done.3, f32[3,4096]{1,0:T(4,128)S(1)} %copy-done.1, f32[2,2,128,128]{3,2,1,0:T(8,128)S(1)} %copy-done, f32[1,4096]{1,0:T(1,128)S(1)} %bitcast.3), custom_call_target="tpu_custom_call" | custom-call | tf_op jit(solution)/shard_map/map_fit/pallas_call | solution.py:293
  130.2 0.6 copy.7
Async XLA Ops:
  0.0 0.7 copy-start.4
  0.7 0.9 copy-start
  1.6 0.8 copy-start.1
  2.4 0.7 copy-start.2
  3.2 0.7 copy-start.3

commit v2 on v1

v2 whole, which is shorter than its diff:
```python
import functools
import math

import jax
import jax.numpy as jnp
from jax import lax
from jax.experimental import pallas as pl
from jax.experimental.pallas import tpu as pltpu
from jax.sharding import PartitionSpec as P

ITERS = 2
GRID_Y = 4
NEAR = 4

HEIGHT = 2.5
REFERENCE_RANGE = 2.5
TURN_STEP = 25.0 / 343.0
HALF_PI = math.pi / 2.0

MESH = pl.DeviceIdType.MESH
F32 = jnp.float32
BF16 = jnp.bfloat16

SIN_COEFFS = (3.141590270, -5.167406733, 2.544010518, -0.559462455)
COS_COEFFS = (0.999993249, -4.933934668, 4.041248102, -1.222031763)


def horner(coeffs, u):
    value = coeffs[-1]
    for c in coeffs[-2::-1]:
        value = value * u + c
    return value


def kernel(
    grid_size,
    freq_size,
    bins_hbm,
    mics_hbm,
    points_hbm,
    cross_hbm,
    start_hbm,
    out_ref,
    bins_ref,
    mics_ref,
    points_ref,
    cross_ref,
    strength,
    mic_cols,
    steer,
    gram,
    scattered,
    arrived,
    far,
    gather,
    grads,
    norms,
    parts_a,
    parts_b,
    load_sem,
    send_sem,
    recv_sem,
):
    nb = bins_ref.shape[0]
    mics = mics_ref.shape[1]
    points = points_ref.shape[1]
    ny = GRID_Y
    nz = grid_size // ny
    far_size = nz // NEAR
    chunks = ny * NEAR
    rows = mics // chunks
    total = points * grid_size
    inverse = 1.0 / total

    g = lax.axis_index("grid")
    f = lax.axis_index("freq")
    y, z = lax.div(g, nz), lax.rem(g, nz)
    chunk_id = y * NEAR + lax.rem(z, NEAR)
    far_id = lax.div(z, NEAR)

    def at(y_id, z_id, f_id):
        return {"grid": y_id * nz + z_id, "freq": f_id}

    def near(reach):
        peers = []
        for dy in range(ny):
            y_id = lax.rem(y + dy, ny)
            for dz in reach:
                if dy == 0 and isinstance(dz, int) and dz == 0:
                    continue
                z_id = lax.rem(z + dz + nz, nz)
                peers.append((y_id * NEAR + lax.rem(z_id, NEAR), at(y_id, z_id, f)))
        return peers

    two = 2 - 4 * lax.rem(f, 2)
    owners = near((0, 1, -1, two))
    clients = near((0, 1, -1, -two))
    neighbours = near((0, 1, -1, 2, -2))
    far_peers = [at(y, lax.rem(z + d * NEAR, nz), f) for d in range(1, far_size)]
    f_peers = [at(y, z, lax.rem(f + d, freq_size)) for d in range(1, freq_size)]

    loads = [
        pltpu.make_async_copy(src, dst, load_sem.at[i])
        for i, (src, dst) in enumerate(
            (
                (bins_hbm, bins_ref),
                (mics_hbm, mics_ref),
                (points_hbm, points_ref),
                (start_hbm, strength),
                (cross_hbm, cross_ref),
            )
        )
    ]
    for load in loads:
        load.start()

    greeted = [peer for _, peer in neighbours] + far_peers + f_peers
    barrier = pltpu.get_barrier_semaphore()
    for peer in greeted:
        pl.semaphore_signal(barrier, inc=1, device_id=peer, device_id_type=MESH)

    unsent = []

    def begin(phase, copies, like):
        for src, dst, peer in copies:
            pltpu.make_async_remote_copy(
                src_ref=src,
                dst_ref=dst,
                send_sem=send_sem.at[phase],
                recv_sem=recv_sem.at[phase],
                device_id=peer,
                device_id_type=MESH,
            ).start()
        if copies:
            unsent.append((phase, like))

    def finish(phase, copies, like):
        if copies:
            pltpu.make_async_copy(like, like, recv_sem.at[phase]).wait()

    def exchange(phase, copies, like):
        begin(phase, copies, like)
        finish(phase, copies, like)

    for load in loads[:3]:
        load.wait()

    for axis in range(3):
        mic_cols[axis] = jnp.transpose(jnp.broadcast_to(mics_ref[axis : axis + 1, :], (mics, mics)))
    scale = [bins_ref[b].astype(F32) * TURN_STEP for b in range(nb)]
    sub, lanes = 16, 512
    blocks_m = mics // sub

    def steer_block(i, carry):
        m0 = pl.multiple_of(lax.rem(i, blocks_m) * sub, sub)
        c0 = pl.multiple_of(lax.div(i, blocks_m) * lanes, lanes)
        cols = pl.ds(c0, lanes)

        def mic(axis):
            tile = mic_cols[axis, pl.ds(m0, sub), :]
            return jnp.concatenate([tile] * (lanes // mics), axis=1)

        dx = points_ref[0:1, cols] - mic(0)
        dy = points_ref[1:2, cols] - mic(1)
        dz = (points_ref[2:3, cols] + HEIGHT) - mic(2)
        square = dx * dx + dy * dy + dz * dz
        inv = lax.rsqrt(square)
        inv = inv * (1.5 - 0.5 * square * inv * inv)
        distance = square * inv
        amplitude = REFERENCE_RANGE * inv
        for b in range(nb):
            turns = distance * scale[b]
            frac = turns - jnp.round(turns)
            u = frac * frac
            half_sin = frac * horner(SIN_COEFFS, u)
            half_cos = horner(COS_COEFFS, u)
            twice = (2.0 * amplitude) * half_sin
            real = amplitude - twice * half_sin
            imag = -(twice * half_cos)
            steer[b, pl.ds(m0, sub), cols] = real.astype(BF16)
            steer[b, pl.ds(m0 + mics, sub), cols] = imag.astype(BF16)
        return carry

    lax.fori_loop(0, blocks_m * (points // lanes), steer_block, 0)

    row = lax.broadcasted_iota(jnp.int32, (mics, mics), 0)
    col = lax.broadcasted_iota(jnp.int32, (mics, mics), 1)
    upper = row <= col
    diagonal = row == col

    def gram_of(b, weights):
        s = steer[b]
        gram[b] = lax.dot_general(
            (s.astype(F32) * weights).astype(BF16),
            s,
            (((1,), (1,)), ((), ())),
            preferred_element_type=F32,
        )
        real = gram[b, :mics, :mics] + gram[b, mics:, mics:]
        imag = gram[b, mics:, :mics] - gram[b, :mics, mics:]
        return jnp.where(upper, real, imag)

    def summed(slot, phase, weights):
        for b in range(nb):
            scattered[slot, :, b] = gram_of(b, weights).reshape(chunks, rows, mics)
        if slot == 0:
            pl.semaphore_wait(barrier, len(greeted))
        exchange(
            phase,
            [
                (scattered.at[slot, k], arrived.at[slot, i], peer)
                for i, (k, peer) in enumerate(owners)
            ],
            arrived.at[slot],
        )
        far[slot, far_id] = scattered[slot, chunk_id] + jnp.sum(arrived[slot], axis=0)
        exchange(
            phase + 1,
            [(far.at[slot, far_id], far.at[slot, far_id], peer) for peer in far_peers],
            far.at[slot, pl.ds(0, far_size - 1)],
        )
        return jnp.sum(far[slot], axis=0)

    for it in range(ITERS):
        base = 9 * it

        if it == 0:
            loads[3].wait()
        gather[it, chunk_id] = summed(2 * it, base, strength[...])
        exchange(
            base + 2,
            [(gather.at[it, chunk_id], gather.at[it, chunk_id], peer) for _, peer in clients],
            gather.at[it, pl.ds(0, chunks - 1)],
        )
        if it == 0:
            loads[4].wait()
        operators = []
        for b in range(nb):
            model = gather[it, :, b].reshape(mics, mics)
            flipped = jnp.transpose(model)
            model_real = jnp.where(upper, model, flipped)
            model_imag = jnp.where(diagonal, 0.0, jnp.where(upper, -flipped, model))
            res_real = cross_ref[b, 0] - model_real * inverse
            res_imag = cross_ref[b, 1] - model_imag * inverse
            operators.append(
                jnp.concatenate(
                    [
                        jnp.concatenate([res_real, -res_imag], axis=1),
                        jnp.concatenate([res_imag, res_real], axis=1),
                    ],
                    axis=0,
                ).astype(BF16)
            )

        width = 512
        for k in range(points // width):
            cols = pl.ds(k * width, width)
            term = None
            for b in range(nb):
                s = steer[b, :, cols]
                applied = jnp.dot(operators[b], s, preferred_element_type=F32)
                product = (s.astype(F32) * applied).reshape(2 * mics // 8, 8, width)
                product = jnp.sum(product, axis=0)
                term = product if term is None else term + product
            grads[it, f, :, cols] = jnp.sum(term, axis=0, keepdims=True)
        exchange(
            base + 3,
            [(grads.at[it, f], grads.at[it, f], peer) for peer in f_peers],
            grads.at[it, pl.ds(0, freq_size - 1)],
        )
        gradient = grads[it, 0]
        for j in range(1, freq_size):
            gradient = gradient + grads[it, j]
        gradient = (-2.0 * inverse) * gradient
        squares = gradient * gradient
        normed = squares[:, :mics]
        for k in range(1, points // mics):
            normed = normed + squares[:, k * mics : (k + 1) * mics]
        norms[it, far_id] = normed * (1.0 / freq_size)
        norm_copies = [(norms.at[it, far_id], norms.at[it, far_id], peer) for peer in far_peers]
        norm_like = norms.at[it, pl.ds(0, far_size - 1)]
        begin(base + 4, norm_copies, norm_like)

        mine = summed(2 * it + 1, base + 5, gradient) * inverse
        index = lax.broadcasted_iota(jnp.int32, (nb, rows, mics), 1) + chunk_id * rows
        column = lax.broadcasted_iota(jnp.int32, (nb, rows, mics), 2)
        curved = mine * mine * jnp.where(index == column, 1.0, 2.0)
        curved = jnp.sum(jnp.sum(curved, axis=0), axis=0, keepdims=True)
        finish(base + 4, norm_copies, norm_like)
        parts_a[it, f] = jnp.concatenate([jnp.sum(norms[it], axis=0), curved], axis=0)
        exchange(
            base + 7,
            [(parts_a.at[it, f], parts_a.at[it, f], peer) for peer in f_peers],
            parts_a.at[it, pl.ds(0, freq_size - 1)],
        )
        parts_b[it, chunk_id] = jnp.sum(parts_a[it], axis=0)
        exchange(
            base + 8,
            [(parts_b.at[it, chunk_id], parts_b.at[it, chunk_id], peer) for _, peer in clients],
            parts_b.at[it, pl.ds(0, chunks - 1)],
        )
        sums = jnp.sum(jnp.sum(parts_b[it], axis=0), axis=1, keepdims=True)
        step_length = 0.5 * sums[0:1] / sums[1:2]
        updated = jnp.maximum(strength[...] - step_length * gradient, 0.0)
        if it < ITERS - 1:
            strength[...] = updated
        else:
            out_ref[...] = updated

    for phase, like in unsent:
        pltpu.make_async_copy(like, like, send_sem.at[phase]).wait()


def local(grid_size, freq_size, bin_index, microphones, grid_points, cross_spectra, initial_strengths):
    nb = bin_index.shape[0]
    mics = microphones.shape[1]
    points = grid_points.shape[1]
    ny = GRID_Y
    nz = grid_size // ny
    far_size = nz // NEAR
    chunks = ny * NEAR
    rows = mics // chunks
    hbm = pl.BlockSpec(memory_space=pltpu.HBM)
    out = pl.pallas_call(
        functools.partial(kernel, grid_size, freq_size),
        out_shape=jax.ShapeDtypeStruct((1, points), F32),
        in_specs=[hbm] * 5,
        out_specs=pl.BlockSpec(memory_space=pltpu.VMEM),
        scratch_shapes=[
            pltpu.SMEM((nb,), jnp.int32),
            pltpu.VMEM((3, mics), F32),
            pltpu.VMEM((3, points), F32),
            pltpu.VMEM((nb, 2, mics, mics), F32),
            pltpu.VMEM((1, points), F32),
            pltpu.VMEM((3, mics, mics), F32),
            pltpu.VMEM((nb, 2 * mics, points), BF16),
            pltpu.VMEM((nb, 2 * mics, 2 * mics), F32),
            pltpu.VMEM((2 * ITERS, chunks, nb, rows, mics), F32),
            pltpu.VMEM((2 * ITERS, chunks - 1, nb, rows, mics), F32),
            pltpu.VMEM((2 * ITERS, far_size, nb, rows, mics), F32),
            pltpu.VMEM((ITERS, chunks, nb, rows, mics), F32),
            pltpu.VMEM((ITERS, freq_size, 1, points), F32),
            pltpu.VMEM((ITERS, far_size, 1, mics), F32),
            pltpu.VMEM((ITERS, freq_size, 2, mics), F32),
            pltpu.VMEM((ITERS, chunks, 2, mics), F32),
            pltpu.SemaphoreType.DMA((5,)),
            pltpu.SemaphoreType.DMA((9 * ITERS,)),
            pltpu.SemaphoreType.DMA((9 * ITERS,)),
        ],
        compiler_params=pltpu.CompilerParams(
            collective_id=0, has_side_effects=True, vmem_limit_bytes=48 * 1024 * 1024
        ),
        name="map_fit",
    )(bin_index, microphones, grid_points, cross_spectra, initial_strengths.reshape(1, points))
    return out.reshape(points)


def solution(mesh):
    placed = (P("freq"), P(), P(None, "grid"), P("freq", None, None, None), P("grid"))
    body = functools.partial(local, mesh.shape["grid"], mesh.shape["freq"])
    return jax.shard_map(body, mesh=mesh, in_specs=placed, out_specs=P("grid"), check_vma=False)
```

time: 131 us -> 115 us (0.88)
  Pallas kernels: 126 us -> 110 us
    pallas_call x1, Pallas kernels: 126 us -> 110 us  [local(): pl.pallas_call(functools.partial(kernel, grid_size, freq_size), out_shape...]
where the time goes in v2:
time: 115 us; the launch traced here: 114 us
  Pallas kernels  110 us (96%)
  local copies, waits for them, and re-layouts  4.45 us (4%)
    pallas_call x1, Pallas kernels, local(): pl.pallas_call(functools.partial(kernel, grid_size, freq_size), out_shape...  110 us
    unnamed x11, local copies, waits for them, and re-layouts  4.45 us

profile of v2, /device:TPU:1, one launch (start us, length us, event | category | flops | bytes accessed | tf_op | source)
XLA Modules:
  0.0 114.4 jit_solution(17351322071866374536)
XLA Ops:
  0.0 0.0 copy-start.4
  0.0 0.7 copy-done.4
  0.7 0.0 copy-start
  0.7 0.9 copy-done
  1.6 0.0 copy-start.1
  1.6 0.8 copy-done.1
  2.4 0.0 copy-start.2
  2.4 0.7 copy-done.2
  3.2 0.0 copy-start.3
  3.2 0.7 copy-done.3
  3.8 109.9 %map_fit.1 = f32[1,4096]{1,0:T(1,128)S(1)} custom-call(s32[2]{0:T(128)S(1)} %copy-done.4, f32[3,128]{1,0:T(4,128)S(1)} %copy-done.3, f32[3,4096]{1,0:T(4,128)S(1)} %copy-done.1, f32[2,2,128,128]{3,2,1,0:T(8,128)S(1)} %copy-done, f32[1,4096]{1,0:T(1,128)S(1)} %bitcast.3), custom_call_target="tpu_custom_call" | custom-call | tf_op jit(solution)/shard_map/map_fit/pallas_call | solution.py:324
  113.8 0.6 copy.7
Async XLA Ops:
  0.0 0.7 copy-start.4
  0.7 0.9 copy-start
  1.6 0.8 copy-start.1
  2.4 0.7 copy-start.2
  3.2 0.7 copy-start.3

commit v3 on v2

--- a/solution.py
+++ b/solution.py
@@ -10,6 +10,7 @@
 
 ITERS = 2
 GRID_Y = 4
+CORES = 2
 NEAR = 4
 
 HEIGHT = 2.5
@@ -75,29 +76,44 @@
     g = lax.axis_index("grid")
     f = lax.axis_index("freq")
     y, z = lax.div(g, nz), lax.rem(g, nz)
+    cols_x = freq_size // CORES
+    x, core = lax.div(f, CORES), lax.rem(f, CORES)
     chunk_id = y * NEAR + lax.rem(z, NEAR)
     far_id = lax.div(z, NEAR)
 
     def at(y_id, z_id, f_id):
         return {"grid": y_id * nz + z_id, "freq": f_id}
 
-    def near(reach):
+    def near(reach, x_reach=(0,)):
+        steps = [
+            (min(dx, cols_x - dx) + min(dy, ny - dy) + hops, dx, dy, dz)
+            for dx in x_reach
+            for dy in range(ny)
+            for hops, dz in reach
+        ]
         peers = []
-        for dy in range(ny):
+        for hops, dx, dy, dz in sorted(steps, key=lambda step: -step[0]):
+            if hops == 0:
+                continue
             y_id = lax.rem(y + dy, ny)
-            for dz in reach:
-                if dy == 0 and isinstance(dz, int) and dz == 0:
-                    continue
-                z_id = lax.rem(z + dz + nz, nz)
-                peers.append((y_id * NEAR + lax.rem(z_id, NEAR), at(y_id, z_id, f)))
+            z_id = lax.rem(z + dz + nz, nz)
+            f_id = lax.rem(x + dx, cols_x) * CORES + core
+            peers.append((y_id * NEAR + lax.rem(z_id, NEAR), at(y_id, z_id, f_id)))
         return peers
 
-    two = 2 - 4 * lax.rem(f, 2)
-    owners = near((0, 1, -1, two))
-    clients = near((0, 1, -1, -two))
-    neighbours = near((0, 1, -1, 2, -2))
-    far_peers = [at(y, lax.rem(z + d * NEAR, nz), f) for d in range(1, far_size)]
-    f_peers = [at(y, z, lax.rem(f + d, freq_size)) for d in range(1, freq_size)]
+    two = 2 - 4 * core
+    owners = near(((0, 0), (1, 1), (1, -1), (2, two)))
+    clients = near(((0, 0), (1, 1), (1, -1), (2, -two)))
+    all_x = tuple(range(1, cols_x))
+    clients_x = near(((0, 0), (1, 1), (1, -1), (2, -two)), (0,) + all_x)
+    owners_x = near(((0, 0), (1, 1), (1, -1), (2, two)), all_x)
+    neighbours = near(((0, 0), (1, 1), (1, -1), (2, 2), (2, -2)))
+    far_peers = [at(y, lax.rem(z + d * NEAR, nz), f) for d in (2, 1, 3) if d < far_size]
+    other_core = at(y, z, x * CORES + 1 - core)
+    f_steps = [(dx, dc) for dx in (2, 1, 3) if dx < cols_x for dc in (1, 0)] + [(0, 1)]
+    f_peers = [
+        at(y, z, lax.rem(x + dx, cols_x) * CORES + lax.rem(core + dc, CORES)) for dx, dc in f_steps
+    ]
 
     loads = [
         pltpu.make_async_copy(src, dst, load_sem.at[i])
@@ -114,7 +130,7 @@
     for load in loads:
         load.start()
 
-    greeted = [peer for _, peer in neighbours] + far_peers + f_peers
+    greeted = [peer for _, peer in neighbours] + far_peers + f_peers + [peer for _, peer in owners_x]
     barrier = pltpu.get_barrier_semaphore()
     for peer in greeted:
         pl.semaphore_signal(barrier, inc=1, device_id=peer, device_id_type=MESH)
@@ -287,17 +303,18 @@
         curved = mine * mine * jnp.where(index == column, 1.0, 2.0)
         curved = jnp.sum(jnp.sum(curved, axis=0), axis=0, keepdims=True)
         finish(base + 4, norm_copies, norm_like)
-        parts_a[it, f] = jnp.concatenate([jnp.sum(norms[it], axis=0), curved], axis=0)
+        parts_a[it, core] = jnp.concatenate([jnp.sum(norms[it], axis=0), curved], axis=0)
         exchange(
             base + 7,
-            [(parts_a.at[it, f], parts_a.at[it, f], peer) for peer in f_peers],
-            parts_a.at[it, pl.ds(0, freq_size - 1)],
-        )
-        parts_b[it, chunk_id] = jnp.sum(parts_a[it], axis=0)
+            [(parts_a.at[it, core], parts_a.at[it, core], other_core)],
+            parts_a.at[it, 0],
+        )
+        own = x * chunks + chunk_id
+        parts_b[it, own] = jnp.sum(parts_a[it], axis=0)
         exchange(
             base + 8,
-            [(parts_b.at[it, chunk_id], parts_b.at[it, chunk_id], peer) for _, peer in clients],
-            parts_b.at[it, pl.ds(0, chunks - 1)],
+            [(parts_b.at[it, own], parts_b.at[it, own], peer) for _, peer in clients_x],
+            parts_b.at[it, pl.ds(0, cols_x * chunks - 1)],
         )
         sums = jnp.sum(jnp.sum(parts_b[it], axis=0), axis=1, keepdims=True)
         step_length = 0.5 * sums[0:1] / sums[1:2]
@@ -341,14 +358,14 @@
             pltpu.VMEM((ITERS, chunks, nb, rows, mics), F32),
             pltpu.VMEM((ITERS, freq_size, 1, points), F32),
             pltpu.VMEM((ITERS, far_size, 1, mics), F32),
-            pltpu.VMEM((ITERS, freq_size, 2, mics), F32),
-            pltpu.VMEM((ITERS, chunks, 2, mics), F32),
+            pltpu.VMEM((ITERS, CORES, 2, mics), F32),
+            pltpu.VMEM((ITERS, freq_size // CORES * chunks, 2, mics), F32),
             pltpu.SemaphoreType.DMA((5,)),
             pltpu.SemaphoreType.DMA((9 * ITERS,)),
             pltpu.SemaphoreType.DMA((9 * ITERS,)),
         ],
         compiler_params=pltpu.CompilerParams(
-            collective_id=0, has_side_effects=True, vmem_limit_bytes=48 * 1024 * 1024
+            collective_id=0, has_side_effects=True, vmem_limit_bytes=62 * 1024 * 1024
         ),
         name="map_fit",
     )(bin_index, microphones, grid_points, cross_spectra, initial_strengths.reshape(1, points))

time: 115 us -> 107 us (0.930)
  Pallas kernels: 110 us -> 105 us
  local copies, waits for them, and re-layouts: 4.45 us -> 1.32 us
    pallas_call x1, Pallas kernels: 110 us -> 105 us  [local(): pl.pallas_call(functools.partial(kernel, grid_size, freq_size), out_shape...]
    unnamed x11 -> x1, local copies, waits for them, and re-layouts: 4.45 us -> 1.32 us
where the time goes in v3:
time: 107 us; the launch traced here: 106 us
  Pallas kernels  105 us (98%)
  local copies, waits for them, and re-layouts  1.32 us (1%)
    pallas_call x1, Pallas kernels, local(): pl.pallas_call(functools.partial(kernel, grid_size, freq_size), out_shape...  105 us

profile of v3, /device:TPU:1, one launch (start us, length us, event | category | flops | bytes accessed | tf_op | source)
XLA Modules:
  0.0 106.4 jit_solution(17698571344744911815)
XLA Ops:
  0.0 105.0 %map_fit.1 = f32[1,4096]{1,0:T(1,128)} custom-call(s32[2]{0:T(128)} %bins_hbm.1, f32[3,128]{1,0:T(4,128)} %mics_hbm.1, f32[3,4096]{1,0:T(4,128)} %points_hbm.1, f32[2,2,128,128]{3,2,1,0:T(8,128)} %cross_hbm.1, f32[1,4096]{1,0:T(1,128)} %bitcast.3), custom_call_target="tpu_custom_call" | custom-call | tf_op jit(solution)/shard_map/map_fit/pallas_call | solution.py:341
  105.0 1.3 %copy.7 = f32[4096]{0:T(1024)} copy(f32[4096]{0:T(1024)} %bitcast.2) | data formatting | bytes 32768

commit v4 on v3

--- a/solution.py
+++ b/solution.py
@@ -11,6 +11,8 @@
 ITERS = 2
 GRID_Y = 4
 CORES = 2
+HALVES = 2
+PHASES = 16
 NEAR = 4
 
 HEIGHT = 2.5
@@ -54,6 +56,7 @@
     arrived,
     far,
     gather,
+    terms,
     grads,
     norms,
     parts_a,
@@ -204,125 +207,168 @@
     upper = row <= col
     diagonal = row == col
 
-    def gram_of(b, weights):
-        s = steer[b]
-        gram[b] = lax.dot_general(
+    def product(b, cols, weights):
+        s = steer[b, :, cols]
+        return lax.dot_general(
             (s.astype(F32) * weights).astype(BF16),
             s,
             (((1,), (1,)), ((), ())),
             preferred_element_type=F32,
         )
+
+    def scatter(slot, b, phase):
         real = gram[b, :mics, :mics] + gram[b, mics:, mics:]
         imag = gram[b, mics:, :mics] - gram[b, :mics, mics:]
-        return jnp.where(upper, real, imag)
-
-    def summed(slot, phase, weights):
-        for b in range(nb):
-            scattered[slot, :, b] = gram_of(b, weights).reshape(chunks, rows, mics)
-        if slot == 0:
-            pl.semaphore_wait(barrier, len(greeted))
-        exchange(
+        scattered[slot, b] = jnp.where(upper, real, imag).reshape(chunks, rows, mics)
+        begin(
             phase,
             [
-                (scattered.at[slot, k], arrived.at[slot, i], peer)
+                (scattered.at[slot, b, k], arrived.at[slot, b, i], peer)
                 for i, (k, peer) in enumerate(owners)
             ],
-            arrived.at[slot],
+            arrived.at[slot, b],
         )
-        far[slot, far_id] = scattered[slot, chunk_id] + jnp.sum(arrived[slot], axis=0)
-        exchange(
-            phase + 1,
-            [(far.at[slot, far_id], far.at[slot, far_id], peer) for peer in far_peers],
-            far.at[slot, pl.ds(0, far_size - 1)],
-        )
-        return jnp.sum(far[slot], axis=0)
+
+    def swap(slot, b, phase):
+        finish(phase, owners, arrived.at[slot, b])
+        far[slot, b, far_id] = scattered[slot, b, chunk_id] + jnp.sum(arrived[slot, b], axis=0)
+        mine = far.at[slot, b, far_id]
+        begin(phase + nb, [(mine, mine, peer) for peer in far_peers], far.at[slot, b, pl.ds(0, far_size - 1)])
+
+    def summed(slot, b, phase):
+        finish(phase + nb, far_peers, far.at[slot, b, pl.ds(0, far_size - 1)])
+        return jnp.sum(far[slot, b], axis=0)
+
+    bins = range(nb)
+    half = points // HALVES
+    halves = [pl.ds(h * half, half) for h in range(HALVES)]
+    width = 512
+    index = lax.broadcasted_iota(jnp.int32, (rows, mics), 0) + chunk_id * rows
+    column = lax.broadcasted_iota(jnp.int32, (rows, mics), 1)
+    twice = jnp.where(index == column, 1.0, 2.0)
 
     for it in range(ITERS):
-        base = 9 * it
+        base = PHASES * it
+        model_phase = base
+        gather_phase = model_phase + 2 * nb
+        gradient_phase = gather_phase + nb
+        norm_phase = gradient_phase + HALVES
+        direction_phase = norm_phase + 1
+        core_phase = direction_phase + 2 * nb
 
         if it == 0:
             loads[3].wait()
-        gather[it, chunk_id] = summed(2 * it, base, strength[...])
-        exchange(
-            base + 2,
-            [(gather.at[it, chunk_id], gather.at[it, chunk_id], peer) for _, peer in clients],
-            gather.at[it, pl.ds(0, chunks - 1)],
-        )
+        for b in bins:
+            gram[b] = product(b, slice(None), strength[...])
+            if it == 0 and b == 0:
+                pl.semaphore_wait(barrier, len(greeted))
+            scatter(2 * it, b, model_phase + b)
+        for b in bins:
+            swap(2 * it, b, model_phase + b)
+        for b in bins:
+            gather[it, b, chunk_id] = summed(2 * it, b, model_phase + b)
+            mine = gather.at[it, b, chunk_id]
+            begin(
+                gather_phase + b,
+                [(mine, mine, peer) for _, peer in clients],
+                gather.at[it, b, pl.ds(0, chunks - 1)],
+            )
         if it == 0:
             loads[4].wait()
-        operators = []
-        for b in range(nb):
-            model = gather[it, :, b].reshape(mics, mics)
+
+        for b in bins:
+            finish(gather_phase + b, clients, gather.at[it, b, pl.ds(0, chunks - 1)])
+            model = gather[it, b].reshape(mics, mics)
             flipped = jnp.transpose(model)
             model_real = jnp.where(upper, model, flipped)
             model_imag = jnp.where(diagonal, 0.0, jnp.where(upper, -flipped, model))
             res_real = cross_ref[b, 0] - model_real * inverse
             res_imag = cross_ref[b, 1] - model_imag * inverse
-            operators.append(
-                jnp.concatenate(
-                    [
-                        jnp.concatenate([res_real, -res_imag], axis=1),
-                        jnp.concatenate([res_imag, res_real], axis=1),
-                    ],
-                    axis=0,
-                ).astype(BF16)
-            )
-
-        width = 512
-        for k in range(points // width):
-            cols = pl.ds(k * width, width)
-            term = None
-            for b in range(nb):
+            operator = jnp.concatenate(
+                [
+                    jnp.concatenate([res_real, -res_imag], axis=1),
+                    jnp.concatenate([res_imag, res_real], axis=1),
+                ],
+                axis=0,
+            ).astype(BF16)
+            for k in range(points // width):
+                cols = pl.ds(k * width, width)
                 s = steer[b, :, cols]
-                applied = jnp.dot(operators[b], s, preferred_element_type=F32)
-                product = (s.astype(F32) * applied).reshape(2 * mics // 8, 8, width)
-                product = jnp.sum(product, axis=0)
-                term = product if term is None else term + product
-            grads[it, f, :, cols] = jnp.sum(term, axis=0, keepdims=True)
-        exchange(
-            base + 3,
-            [(grads.at[it, f], grads.at[it, f], peer) for peer in f_peers],
-            grads.at[it, pl.ds(0, freq_size - 1)],
-        )
-        gradient = grads[it, 0]
-        for j in range(1, freq_size):
-            gradient = gradient + grads[it, j]
-        gradient = (-2.0 * inverse) * gradient
-        squares = gradient * gradient
-        normed = squares[:, :mics]
-        for k in range(1, points // mics):
-            normed = normed + squares[:, k * mics : (k + 1) * mics]
+                applied = jnp.dot(operator, s, preferred_element_type=F32)
+                term = (s.astype(F32) * applied).reshape(2 * mics // 8, 8, width)
+                term = jnp.sum(term, axis=0)
+                if b > 0:
+                    term = term + terms[:, cols]
+                if b < nb - 1:
+                    terms[:, cols] = term
+                    continue
+                h, offset = k * width // half, k * width % half
+                grads[it, h, f, :, pl.ds(offset, width)] = jnp.sum(term, axis=0, keepdims=True)
+                if offset + width == half:
+                    mine = grads.at[it, h, f]
+                    begin(
+                        gradient_phase + h,
+                        [(mine, mine, peer) for peer in f_peers],
+                        grads.at[it, h, pl.ds(0, freq_size - 1)],
+                    )
+
+        parts = []
+        for h in range(HALVES):
+            finish(gradient_phase + h, f_peers, grads.at[it, h, pl.ds(0, freq_size - 1)])
+            part = grads[it, h, 0]
+            for j in range(1, freq_size):
+                part = part + grads[it, h, j]
+            part = (-2.0 * inverse) * part
+            parts.append(part)
+            for b in bins:
+                if h == 0:
+                    gram[b] = product(b, halves[h], part)
+                else:
+                    gram[b] += product(b, halves[h], part)
+                if h == HALVES - 1:
+                    scatter(2 * it + 1, b, direction_phase + b)
+        normed = None
+        for part in parts:
+            squares = part * part
+            for k in range(half // mics):
+                piece = squares[:, k * mics : (k + 1) * mics]
+                normed = piece if normed is None else normed + piece
         norms[it, far_id] = normed * (1.0 / freq_size)
         norm_copies = [(norms.at[it, far_id], norms.at[it, far_id], peer) for peer in far_peers]
         norm_like = norms.at[it, pl.ds(0, far_size - 1)]
-        begin(base + 4, norm_copies, norm_like)
-
-        mine = summed(2 * it + 1, base + 5, gradient) * inverse
-        index = lax.broadcasted_iota(jnp.int32, (nb, rows, mics), 1) + chunk_id * rows
-        column = lax.broadcasted_iota(jnp.int32, (nb, rows, mics), 2)
-        curved = mine * mine * jnp.where(index == column, 1.0, 2.0)
-        curved = jnp.sum(jnp.sum(curved, axis=0), axis=0, keepdims=True)
-        finish(base + 4, norm_copies, norm_like)
-        parts_a[it, core] = jnp.concatenate([jnp.sum(norms[it], axis=0), curved], axis=0)
+        begin(norm_phase, norm_copies, norm_like)
+
+        for b in bins:
+            swap(2 * it + 1, b, direction_phase + b)
+        finish(norm_phase, norm_copies, norm_like)
+        norm_part = jnp.sum(norms[it], axis=0)
+        curved = None
+        for b in bins:
+            mine = summed(2 * it + 1, b, direction_phase + b) * inverse
+            mine = mine * mine * twice
+            curved = mine if curved is None else curved + mine
+        curved = jnp.sum(curved, axis=0, keepdims=True)
+        parts_a[it, core] = jnp.concatenate([norm_part, curved], axis=0)
         exchange(
-            base + 7,
+            core_phase,
             [(parts_a.at[it, core], parts_a.at[it, core], other_core)],
             parts_a.at[it, 0],
         )
         own = x * chunks + chunk_id
         parts_b[it, own] = jnp.sum(parts_a[it], axis=0)
         exchange(
-            base + 8,
+            core_phase + 1,
             [(parts_b.at[it, own], parts_b.at[it, own], peer) for _, peer in clients_x],
             parts_b.at[it, pl.ds(0, cols_x * chunks - 1)],
         )
         sums = jnp.sum(jnp.sum(parts_b[it], axis=0), axis=1, keepdims=True)
         step_length = 0.5 * sums[0:1] / sums[1:2]
-        updated = jnp.maximum(strength[...] - step_length * gradient, 0.0)
-        if it < ITERS - 1:
-            strength[...] = updated
-        else:
-            out_ref[...] = updated
+        for h in range(HALVES):
+            updated = jnp.maximum(strength[:, halves[h]] - step_length * parts[h], 0.0)
+            if it < ITERS - 1:
+                strength[:, halves[h]] = updated
+            else:
+                out_ref[:, halves[h]] = updated
 
     for phase, like in unsent:
         pltpu.make_async_copy(like, like, send_sem.at[phase]).wait()
@@ -337,6 +383,8 @@
     far_size = nz // NEAR
     chunks = ny * NEAR
     rows = mics // chunks
+    start = initial_strengths.reshape(1, points)
+    arguments = (bin_index, microphones, grid_points, cross_spectra, start)
     hbm = pl.BlockSpec(memory_space=pltpu.HBM)
     out = pl.pallas_call(
         functools.partial(kernel, grid_size, freq_size),
@@ -352,23 +400,24 @@
             pltpu.VMEM((3, mics, mics), F32),
             pltpu.VMEM((nb, 2 * mics, points), BF16),
             pltpu.VMEM((nb, 2 * mics, 2 * mics), F32),
-            pltpu.VMEM((2 * ITERS, chunks, nb, rows, mics), F32),
-            pltpu.VMEM((2 * ITERS, chunks - 1, nb, rows, mics), F32),
-            pltpu.VMEM((2 * ITERS, far_size, nb, rows, mics), F32),
-            pltpu.VMEM((ITERS, chunks, nb, rows, mics), F32),
-            pltpu.VMEM((ITERS, freq_size, 1, points), F32),
+            pltpu.VMEM((2 * ITERS, nb, chunks, rows, mics), F32),
+            pltpu.VMEM((2 * ITERS, nb, chunks - 1, rows, mics), F32),
+            pltpu.VMEM((2 * ITERS, nb, far_size, rows, mics), F32),
+            pltpu.VMEM((ITERS, nb, chunks, rows, mics), F32),
+            pltpu.VMEM((8, points), F32),
+            pltpu.VMEM((ITERS, HALVES, freq_size, 1, points // HALVES), F32),
             pltpu.VMEM((ITERS, far_size, 1, mics), F32),
             pltpu.VMEM((ITERS, CORES, 2, mics), F32),
             pltpu.VMEM((ITERS, freq_size // CORES * chunks, 2, mics), F32),
             pltpu.SemaphoreType.DMA((5,)),
-            pltpu.SemaphoreType.DMA((9 * ITERS,)),
-            pltpu.SemaphoreType.DMA((9 * ITERS,)),
+            pltpu.SemaphoreType.DMA((PHASES * ITERS,)),
+            pltpu.SemaphoreType.DMA((PHASES * ITERS,)),
         ],
         compiler_params=pltpu.CompilerParams(
-            collective_id=0, has_side_effects=True, vmem_limit_bytes=62 * 1024 * 1024
+            collective_id=0, has_side_effects=True, vmem_limit_bytes=48 * 1024 * 1024
         ),
         name="map_fit",
-    )(bin_index, microphones, grid_points, cross_spectra, initial_strengths.reshape(1, points))
+    )(*(pltpu.with_memory_space_constraint(a, pltpu.HBM) for a in arguments))
     return out.reshape(points)
 
 

time: 107 us -> 106 us (level)
  no operation moved by 1% of the time
where the time goes in v4:
time: 106 us
  Pallas kernels  105 us (99%)
    pallas_call x1, Pallas kernels, local(): pl.pallas_call(functools.partial(kernel, grid_size, freq_size), out_shape...  105 us

profile of v4, /device:TPU:1, one launch (start us, length us, event | category | flops | bytes accessed | tf_op | source)
XLA Modules:
  0.0 105.7 jit_solution(2195850057013299268)
XLA Ops:
  0.0 105.0 %map_fit.1 = f32[1,4096]{1,0:T(1,128)S(1)} custom-call(s32[2]{0:T(128)} %bins_hbm.1, f32[3,128]{1,0:T(4,128)} %mics_hbm.1, f32[3,4096]{1,0:T(4,128)} %points_hbm.1, f32[2,2,128,128]{3,2,1,0:T(8,128)} %cross_hbm.1, f32[1,4096]{1,0:T(1,128)} %bitcast.3), custom_call_target="tpu_custom_call" | custom-call | tf_op jit(solution)/shard_map/map_fit/pallas_call | solution.py:389
  105.0 0.6 copy.7
